TPU v7x, 32 devices: a whole 2x2x4 slice. The times are simulated.
32 devices in a mesh: chan: 8 (over y, x, core), freq: 4 (over z).
Axes of the slice: x: 2, y: 2, z: 4, core: 2. Of those that a mesh axis runs over, the one named last changes fastest.
Arguments:
- spectra: bfloat16 [2, 2, 192, 1024], P(None, None, 'freq', 'chan'), may hold values from -1000 to 1000
- masks: int32 [2, 1024], P(None, 'chan'), may hold values 0 or 1
- pair_blocks: int32 [48, 2], P('chan'), may hold values from 0 to 7, as said below
Outputs:
- correlations: bfloat16 [48, 201, 128, 128], P('chan', None, 'freq')
Inputs may be any that keep to these rules, and one draw needn't show every extreme that they name: `pair_blocks`: row p is owned by block p // 6. Its source block (column 0) and receiver block (column 1) differ, and each lies at most 2 blocks from the owner around the closed loop of blocks. In every draw some row has its source exactly 2 blocks below its owner and its receiver exactly 2 above.
All inputs are finite; a program needn't handle non-finite values. No bound on the sum of `masks` on one device may be relied on, other than what follows from the above.
Results may differ from a plain program's by a relative error of at most 0.0068.
Values may be sent and summed in bfloat16 or wider, within the bound.
A program may use at most 128 MiB of HBM per device.

v0:
```python
import math

import jax
import jax.numpy as jnp
from jax import lax
from jax.sharding import PartitionSpec as P

REACH = 2
LAGS = 201


epsilon = 1e-06


def from_behind(value, axis, steps):
    count = lax.axis_size(axis)
    pairs = [(source, (source + steps) % count) for source in range(count)]
    return lax.ppermute(value, axis, pairs)


def lag_table(freq_total, lag_total):
    lag_ids = jnp.arange(lag_total, dtype=jnp.int32) - lag_total // 2
    bin_ids = jnp.arange(freq_total, dtype=jnp.int32)
    phase_index = lag_ids[:, None] * bin_ids[None, :] % (2 * freq_total)
    angles = phase_index.astype(jnp.float32) * (math.pi / freq_total)
    return jnp.concatenate([jnp.cos(angles), -jnp.sin(angles)], axis=1).astype(jnp.bfloat16)


def whiten(values, masks, energy):
    weights = masks.astype(jnp.float32) / jnp.sqrt(energy + epsilon)
    return (values * weights[None, :, None, :]).astype(jnp.bfloat16)


def stack_members(ordered):
    return (
        jnp.stack([member_pair[0] for member_pair in ordered]),
        jnp.stack([member_pair[1] for member_pair in ordered]),
    )


def narrow_neighbours(members):
    below_list = []
    above_list = []
    moving_down = members
    moving_up = members
    for hop_index in range(REACH):
        moving_down = from_behind((moving_down[0], moving_down[1]), "chan", 1)
        moving_up = from_behind((moving_up[0], moving_up[1]), "chan", -1)
        below_list.append(moving_down)
        above_list.append(moving_up)
    return stack_members(below_list[::-1] + [members] + above_list)


def pair_cross(source, receiver, source_mask, receiver_mask):
    real_left = jnp.concatenate([source[0], source[1]], axis=0)
    imag_left = jnp.concatenate([source[1], -source[0]], axis=0)
    left_pair = jnp.stack([real_left, imag_left])
    right_part = jnp.concatenate([receiver[0], receiver[1]], axis=0)
    product = jnp.einsum(
        "ckfi,kfj->cfij", left_pair, right_part, preferred_element_type=jnp.float32
    )
    live_count = jnp.einsum("si,sj->ij", source_mask, receiver_mask)
    product = product / jnp.maximum(live_count, 1.0)
    return product.astype(jnp.bfloat16).reshape(2, product.shape[1], -1)


def all_cross(near_white, near_mask, choosers, row_first, row_count):
    own_rows = lax.dynamic_slice_in_dim(near_white, row_first, row_count, 4)
    mask_rows = lax.dynamic_slice_in_dim(near_mask, row_first, row_count, 2)
    sources = jnp.einsum(
        "pn,nksfi->pksfi", choosers[:, 0], own_rows, preferred_element_type=jnp.float32
    ).astype(jnp.bfloat16)
    receivers = jnp.einsum(
        "pn,nksfj->pksfj", choosers[:, 1], near_white, preferred_element_type=jnp.float32
    ).astype(jnp.bfloat16)
    source_masks = jnp.einsum(
        "pn,nsi->psi", choosers[:, 0], mask_rows, preferred_element_type=jnp.float32
    )
    receiver_masks = jnp.einsum(
        "pn,nsj->psj", choosers[:, 1], near_mask, preferred_element_type=jnp.float32
    )

    def one_pair(members):
        return pair_cross(members[0], members[1], members[2], members[3])

    return lax.map(one_pair, (sources, receivers, source_masks, receiver_masks))


def per_device(spectra, masks, pair_blocks):
    block_width = spectra.shape[3]
    freq_count = lax.axis_size("freq")
    total_bins = spectra.shape[2] * freq_count
    row_count = block_width // freq_count
    row_first = lax.axis_index("freq") * row_count
    own_block = lax.axis_index("chan")
    chan_count = lax.axis_size("chan")
    mask_half = masks.astype(jnp.bfloat16)
    offsets = (pair_blocks - own_block) % chan_count
    offsets = jnp.where(offsets > chan_count // 2, offsets - chan_count, offsets) + REACH
    choosers = (
        offsets[:, :, None] == jnp.arange(2 * REACH + 1, dtype=jnp.int32)[None, None, :]
    ).astype(jnp.bfloat16)
    lag_cosines = lag_table(total_bins, LAGS)
    values = spectra.astype(jnp.float32)
    local_energy = jnp.sum(values[0] * values[0] + values[1] * values[1], axis=1)
    energy = lax.psum(local_energy, "freq") / total_bins
    whitened = whiten(values, masks, energy)
    near_white, near_mask = narrow_neighbours((whitened, mask_half))
    stacked = all_cross(
        lax.all_gather(near_white, "freq", axis=3, tiled=True),
        near_mask,
        choosers,
        row_first,
        row_count,
    )
    pairs_here = stacked.shape[0]
    flattened = stacked.reshape(pairs_here, 2 * total_bins, row_count * block_width)
    lagged = jnp.einsum("lk,pkn->pln", lag_cosines, flattened, preferred_element_type=jnp.float32)
    lagged = lagged * (1.0 / math.sqrt(total_bins))
    return lagged.reshape(pairs_here, LAGS, row_count, block_width).astype(jnp.bfloat16)


def solution(mesh):
    return jax.shard_map(
        per_device,
        mesh=mesh,
        in_specs=(P(None, None, "freq", "chan"), P(None, "chan"), P("chan", None)),
        out_specs=P("chan", None, "freq", None),
        check_vma=False,
    )
```

profile of v0, /device:TPU:0, one launch (start us, length us, event | category | flops | bytes accessed | tf_op | source)
XLA Modules:
  0.0 165.0 jit_solution(2804143515695700852)
XLA Ops:
  0.8 13.5 %psum.7 = f32[2,128]{1,0:T(2,128)S(1)} all-reduce(f32[2,128]{1,0:T(2,128)S(1)} %fusion.13), channel_id=1, replica_groups=mesh['chan'=8,'freq'=4] {'freq'}, use_global_device_ids=true, to_apply=%region_1.2 | all-reduce | flops 256 | bytes 2048 | tf_op jit(solution)/shard_map/psum | solution.py:106
  23.9 2.6 %collective-permute-start.7 = (bf16[2,128]{1,0:T(2,128)(2,1)S(1)}, bf16[2,128]{1,0:T(2,128)(2,1)S(1)}, u32[]{:S(2)}, u32[]{:S(2)}) collective-permute-start(bf16[2,128]{1,0:T(2,128)(2,1)S(1)} %collective-permute-done.6), channel_id=1, source_target_pairs={{0,28},{4,0},{8,4},{12,8},{16,12},{20,16},{24,20},{28,24},{1,29},{... | collective-permute-start | bytes 1544 | tf_op jit(solution)/shard_map/ppermute | solution.py:18
  35.9 27.1 %all_gather.3 = bf16[5,2,2,192,128]{4,0,3,2,1:T(8,128)(2,1)S(1)} all-gather(bf16[5,2,2,48,128]{4,0,3,2,1:T(8,128)(2,1)S(1)} %stack.50), channel_id=1, replica_groups=mesh['chan'=8,'freq'=4] {'freq'}, dimensions={3}, use_global_device_ids=true | all-gather | bytes 1228800 | tf_op jit(solution)/shard_map/all_gather | solution.py:110
  70.2 70.7 %while.10 = (s32[]{:T(128)}, bf16[6,2,192,4096]{3,2,1,0:T(8,128)(2,1)}, bf16[6,2,2,192,128]{4,2,3,1,0:T(2,128)(2,1)}, bf16[6,2,2,192,32]{3,4,2,1,0:T(8,128)(2,1)...) while((s32[]{:T(128)}, ...), condition=%wide.region_3.4_spmd, body=%wide.region_2.3_spmd.sunk | while | flops 16252931 | bytes 17142148 | solution.py:86
  71.9 2.6 %fusion.47 = bf16[2,192,32,128]{3,2,0,1:T(8,128)(2,1)} fusion(f32[32,128]{1,0:T(8,128)S(1)} %convolution_maximum_fusion.2, bf16[2,4,192,32]{3,1,0,2:T(4,128)(2,1)S(1)} %copy.123, bf16[2,192,128]{2,0,1:T(2,128)(2,1)S(1)} %get-tuple-element.147, bf16[2,192,128]{2,0,1:T(2,128)(2,1)S(1)} %get-tuple-element.148), kind=kOutput, calls=%fused_computation.1.clone.1 | convolution fusion | flops 16121856 | bytes 3457024 | tf_op jit(solution)/shard_map/while/body/eval_jaxpr/ckfi,kfj->cfij/dot_general | solution.py:59
  74.5 3.7 %broadcast_in_dim.7 = bf16[1,2,192,4096]{3,1,2,0:T(2,128)(2,1)S(1)} reshape(bf16[2,192,32,128]{3,2,0,1:T(8,128)(2,1)} %fusion.47) | data formatting | bytes 6291456 | tf_op jit(solution)/shard_map/while/body/jit(dynamic_update_index_in_dim)/broadcast_in_dim | solution.py:86
  78.2 3.7 %copy_dynamic-update-slice_fusion.2 = bf16[6,2,192,4096]{3,2,1,0:T(8,128)(2,1)} fusion(bf16[6,2,192,4096]{3,2,1,0:T(8,128)(2,1)} %get-tuple-element.159, s32[]{:T(128)} %get-tuple-element.158, bf16[1,2,192,4096]{3,1,2,0:T(2,128)(2,1)S(1)} %broadcast_in_dim.7), kind=kLoop, calls=%fused_computation.2.clone.1 | loop fusion | bytes 6291968 | tf_op jit(solution)/shard_map/while/body/jit(dynamic_update_index_in_dim)/dynamic_update_slice | solution.py:86
  83.6 2.6 %fusion.47 = bf16[2,192,32,128]{3,2,0,1:T(8,128)(2,1)} fusion(f32[32,128]{1,0:T(8,128)S(1)} %convolution_maximum_fusion.2, bf16[2,4,192,32]{3,1,0,2:T(4,128)(2,1)S(1)} %copy.123, bf16[2,192,128]{2,0,1:T(2,128)(2,1)S(1)} %get-tuple-element.147, bf16[2,192,128]{2,0,1:T(2,128)(2,1)S(1)} %get-tuple-element.148), kind=kOutput, calls=%fused_computation.1.clone.1 | convolution fusion | flops 16121856 | bytes 3457024 | tf_op jit(solution)/shard_map/while/body/eval_jaxpr/ckfi,kfj->cfij/dot_general | solution.py:59
  86.2 3.7 %broadcast_in_dim.7 = bf16[1,2,192,4096]{3,1,2,0:T(2,128)(2,1)S(1)} reshape(bf16[2,192,32,128]{3,2,0,1:T(8,128)(2,1)} %fusion.47) | data formatting | bytes 6291456 | tf_op jit(solution)/shard_map/while/body/jit(dynamic_update_index_in_dim)/broadcast_in_dim | solution.py:86
  90.0 3.8 %copy_dynamic-update-slice_fusion.2 = bf16[6,2,192,4096]{3,2,1,0:T(8,128)(2,1)} fusion(bf16[6,2,192,4096]{3,2,1,0:T(8,128)(2,1)} %get-tuple-element.159, s32[]{:T(128)} %get-tuple-element.158, bf16[1,2,192,4096]{3,1,2,0:T(2,128)(2,1)S(1)} %broadcast_in_dim.7), kind=kLoop, calls=%fused_computation.2.clone.1 | loop fusion | bytes 6291968 | tf_op jit(solution)/shard_map/while/body/jit(dynamic_update_index_in_dim)/dynamic_update_slice | solution.py:86
  95.4 2.6 %fusion.47 = bf16[2,192,32,128]{3,2,0,1:T(8,128)(2,1)} fusion(f32[32,128]{1,0:T(8,128)S(1)} %convolution_maximum_fusion.2, bf16[2,4,192,32]{3,1,0,2:T(4,128)(2,1)S(1)} %copy.123, bf16[2,192,128]{2,0,1:T(2,128)(2,1)S(1)} %get-tuple-element.147, bf16[2,192,128]{2,0,1:T(2,128)(2,1)S(1)} %get-tuple-element.148), kind=kOutput, calls=%fused_computation.1.clone.1 | convolution fusion | flops 16121856 | bytes 3457024 | tf_op jit(solution)/shard_map/while/body/eval_jaxpr/ckfi,kfj->cfij/dot_general | solution.py:59
  98.1 3.7 %broadcast_in_dim.7 = bf16[1,2,192,4096]{3,1,2,0:T(2,128)(2,1)S(1)} reshape(bf16[2,192,32,128]{3,2,0,1:T(8,128)(2,1)} %fusion.47) | data formatting | bytes 6291456 | tf_op jit(solution)/shard_map/while/body/jit(dynamic_update_index_in_dim)/broadcast_in_dim | solution.py:86
  101.8 3.8 %copy_dynamic-update-slice_fusion.2 = bf16[6,2,192,4096]{3,2,1,0:T(8,128)(2,1)} fusion(bf16[6,2,192,4096]{3,2,1,0:T(8,128)(2,1)} %get-tuple-element.159, s32[]{:T(128)} %get-tuple-element.158, bf16[1,2,192,4096]{3,1,2,0:T(2,128)(2,1)S(1)} %broadcast_in_dim.7), kind=kLoop, calls=%fused_computation.2.clone.1 | loop fusion | bytes 6291968 | tf_op jit(solution)/shard_map/while/body/jit(dynamic_update_index_in_dim)/dynamic_update_slice | solution.py:86
  107.3 2.6 %fusion.47 = bf16[2,192,32,128]{3,2,0,1:T(8,128)(2,1)} fusion(f32[32,128]{1,0:T(8,128)S(1)} %convolution_maximum_fusion.2, bf16[2,4,192,32]{3,1,0,2:T(4,128)(2,1)S(1)} %copy.123, bf16[2,192,128]{2,0,1:T(2,128)(2,1)S(1)} %get-tuple-element.147, bf16[2,192,128]{2,0,1:T(2,128)(2,1)S(1)} %get-tuple-element.148), kind=kOutput, calls=%fused_computation.1.clone.1 | convolution fusion | flops 16121856 | bytes 3457024 | tf_op jit(solution)/shard_map/while/body/eval_jaxpr/ckfi,kfj->cfij/dot_general | solution.py:59
  109.9 3.7 %broadcast_in_dim.7 = bf16[1,2,192,4096]{3,1,2,0:T(2,128)(2,1)S(1)} reshape(bf16[2,192,32,128]{3,2,0,1:T(8,128)(2,1)} %fusion.47) | data formatting | bytes 6291456 | tf_op jit(solution)/shard_map/while/body/jit(dynamic_update_index_in_dim)/broadcast_in_dim | solution.py:86
  113.6 3.8 %copy_dynamic-update-slice_fusion.2 = bf16[6,2,192,4096]{3,2,1,0:T(8,128)(2,1)} fusion(bf16[6,2,192,4096]{3,2,1,0:T(8,128)(2,1)} %get-tuple-element.159, s32[]{:T(128)} %get-tuple-element.158, bf16[1,2,192,4096]{3,1,2,0:T(2,128)(2,1)S(1)} %broadcast_in_dim.7), kind=kLoop, calls=%fused_computation.2.clone.1 | loop fusion | bytes 6291968 | tf_op jit(solution)/shard_map/while/body/jit(dynamic_update_index_in_dim)/dynamic_update_slice | solution.py:86
  119.0 2.6 %fusion.47 = bf16[2,192,32,128]{3,2,0,1:T(8,128)(2,1)} fusion(f32[32,128]{1,0:T(8,128)S(1)} %convolution_maximum_fusion.2, bf16[2,4,192,32]{3,1,0,2:T(4,128)(2,1)S(1)} %copy.123, bf16[2,192,128]{2,0,1:T(2,128)(2,1)S(1)} %get-tuple-element.147, bf16[2,192,128]{2,0,1:T(2,128)(2,1)S(1)} %get-tuple-element.148), kind=kOutput, calls=%fused_computation.1.clone.1 | convolution fusion | flops 16121856 | bytes 3457024 | tf_op jit(solution)/shard_map/while/body/eval_jaxpr/ckfi,kfj->cfij/dot_general | solution.py:59
  121.7 3.7 %broadcast_in_dim.7 = bf16[1,2,192,4096]{3,1,2,0:T(2,128)(2,1)S(1)} reshape(bf16[2,192,32,128]{3,2,0,1:T(8,128)(2,1)} %fusion.47) | data formatting | bytes 6291456 | tf_op jit(solution)/shard_map/while/body/jit(dynamic_update_index_in_dim)/broadcast_in_dim | solution.py:86
  125.4 3.7 %copy_dynamic-update-slice_fusion.2 = bf16[6,2,192,4096]{3,2,1,0:T(8,128)(2,1)} fusion(bf16[6,2,192,4096]{3,2,1,0:T(8,128)(2,1)} %get-tuple-element.159, s32[]{:T(128)} %get-tuple-element.158, bf16[1,2,192,4096]{3,1,2,0:T(2,128)(2,1)S(1)} %broadcast_in_dim.7), kind=kLoop, calls=%fused_computation.2.clone.1 | loop fusion | bytes 6291968 | tf_op jit(solution)/shard_map/while/body/jit(dynamic_update_index_in_dim)/dynamic_update_slice | solution.py:86
  130.8 2.6 %fusion.47 = bf16[2,192,32,128]{3,2,0,1:T(8,128)(2,1)} fusion(f32[32,128]{1,0:T(8,128)S(1)} %convolution_maximum_fusion.2, bf16[2,4,192,32]{3,1,0,2:T(4,128)(2,1)S(1)} %copy.123, bf16[2,192,128]{2,0,1:T(2,128)(2,1)S(1)} %get-tuple-element.147, bf16[2,192,128]{2,0,1:T(2,128)(2,1)S(1)} %get-tuple-element.148), kind=kOutput, calls=%fused_computation.1.clone.1 | convolution fusion | flops 16121856 | bytes 3457024 | tf_op jit(solution)/shard_map/while/body/eval_jaxpr/ckfi,kfj->cfij/dot_general | solution.py:59
  133.4 3.7 %broadcast_in_dim.7 = bf16[1,2,192,4096]{3,1,2,0:T(2,128)(2,1)S(1)} reshape(bf16[2,192,32,128]{3,2,0,1:T(8,128)(2,1)} %fusion.47) | data formatting | bytes 6291456 | tf_op jit(solution)/shard_map/while/body/jit(dynamic_update_index_in_dim)/broadcast_in_dim | solution.py:86
  137.2 3.8 %copy_dynamic-update-slice_fusion.2 = bf16[6,2,192,4096]{3,2,1,0:T(8,128)(2,1)} fusion(bf16[6,2,192,4096]{3,2,1,0:T(8,128)(2,1)} %get-tuple-element.159, s32[]{:T(128)} %get-tuple-element.158, bf16[1,2,192,4096]{3,1,2,0:T(2,128)(2,1)S(1)} %broadcast_in_dim.7), kind=kLoop, calls=%fused_computation.2.clone.1 | loop fusion | bytes 6291968 | tf_op jit(solution)/shard_map/while/body/jit(dynamic_update_index_in_dim)/dynamic_update_slice | solution.py:86
  140.9 13.1 %fusion.4 = bf16[6,201,4096]{2,1,0:T(8,128)(2,1)} fusion(bf16[6,384,4096]{2,1,0:T(8,128)(2,1)} %bitcast.104, bf16[201,192]{1,0:T(8,128)(2,1)} %get-tuple-element.99, bf16[201,192]{1,0:T(8,128)(2,1)} %get-tuple-element.98), kind=kOutput, calls=%fused_computation.18 | convolution fusion | flops 3803936256 | bytes 28908288 | tf_op jit(solution)/shard_map/lk,pkn->pln/dot_general | solution.py:118
  154.1 11.0 %convert_element_type.46 = bf16[6,201,32,128]{3,2,1,0:T(8,128)(2,1)} reshape(bf16[6,201,4096]{2,1,0:T(8,128)(2,1)} %fusion.4) | data formatting | bytes 19759104 | tf_op jit(solution)/shard_map/convert_element_type | solution.py:120
  (105 shorter events, 36.5 us)
Async XLA Ops:
  15.8 12.2 %collective-permute-start.2 = (bf16[2,2,48,128]{3,2,1,0:T(8,128)(2,1)S(1)}, bf16[2,2,48,128]{3,2,1,0:T(8,128)(2,1)S(1)}, u32[]{:S(2)}, u32[]{:S(2)}) collective-permute-start(bf16[2,2,48,128]{3,2,1,0:T(8,128)(2,1)S(1)} %multiply_convert_fusion.1), channel_id=1, source_target_pairs={{0,28},{4,0},{8,4},{12,8},{16,12},{20,16},{24,20},{28,24},{1,29},{... | collective-permute-start | bytes 147464 | tf_op jit(solution)/shard_map/ppermute | solution.py:18
  15.9 14.7 %collective-permute-start = (bf16[2,2,48,128]{3,2,1,0:T(8,128)(2,1)S(1)}, bf16[2,2,48,128]{3,2,1,0:T(8,128)(2,1)S(1)}, u32[]{:S(2)}, u32[]{:S(2)}) collective-permute-start(bf16[2,2,48,128]{3,2,1,0:T(8,128)(2,1)S(1)} %multiply_convert_fusion.1), channel_id=1, source_target_pairs={{0,4},{4,8},{8,12},{12,16},{16,20},{20,24},{24,28},{28,0},{1,5},{5... | collective-permute-start | bytes 147464 | tf_op jit(solution)/shard_map/ppermute | solution.py:18
  17.0 6.8 %collective-permute-start.4 = (bf16[2,128]{1,0:T(2,128)(2,1)S(1)}, bf16[2,128]{1,0:T(2,128)(2,1)S(1)}, u32[]{:S(2)}, u32[]{:S(2)}) collective-permute-start(bf16[2,128]{1,0:T(2,128)(2,1)S(1)} %convert_element_type.42), channel_id=1, source_target_pairs={{0,4},{4,8},{8,12},{12,16},{16,20},{20,24},{24,28},{28,0},{1,5},{5... | collective-permute-start | bytes 1544 | tf_op jit(solution)/shard_map/ppermute | solution.py:18
  18.2 5.7 %collective-permute-start.6 = (bf16[2,128]{1,0:T(2,128)(2,1)S(1)}, bf16[2,128]{1,0:T(2,128)(2,1)S(1)}, u32[]{:S(2)}, u32[]{:S(2)}) collective-permute-start(bf16[2,128]{1,0:T(2,128)(2,1)S(1)} %convert_element_type.42), channel_id=1, source_target_pairs={{0,28},{4,0},{8,4},{12,8},{16,12},{20,16},{24,20},{28,24},{1,29},{... | collective-permute-start | bytes 1544 | tf_op jit(solution)/shard_map/ppermute | solution.py:18
  22.0 10.3 %copy-start = (pred[6,2,5]{2,0,1:T(8,128)(4,1)}, pred[6,2,5]{2,0,1:T(8,128)(4,1)S(1)}, u32[]{:S(2)}) copy-start(pred[6,2,5]{2,0,1:T(8,128)(4,1)S(1)} %iota_compare_fusion) | copy-start | bytes 184
  23.8 3.9 %collective-permute-start.5 = (bf16[2,128]{1,0:T(2,128)(2,1)S(1)}, bf16[2,128]{1,0:T(2,128)(2,1)S(1)}, u32[]{:S(2)}, u32[]{:S(2)}) collective-permute-start(bf16[2,128]{1,0:T(2,128)(2,1)S(1)} %collective-permute-done.4), channel_id=1, source_target_pairs={{0,4},{4,8},{8,12},{12,16},{16,20},{20,24},{24,28},{28,0},{1,5},{5... | collective-permute-start | bytes 1544 | tf_op jit(solution)/shard_map/ppermute | solution.py:18
  23.9 3.9 %collective-permute-start.7 = (bf16[2,128]{1,0:T(2,128)(2,1)S(1)}, bf16[2,128]{1,0:T(2,128)(2,1)S(1)}, u32[]{:S(2)}, u32[]{:S(2)}) collective-permute-start(bf16[2,128]{1,0:T(2,128)(2,1)S(1)} %collective-permute-done.6), channel_id=1, source_target_pairs={{0,28},{4,0},{8,4},{12,8},{16,12},{20,16},{24,20},{28,24},{1,29},{... | collective-permute-start | bytes 1544 | tf_op jit(solution)/shard_map/ppermute | solution.py:18
  28.0 4.3 %collective-permute-start.3 = (bf16[2,2,48,128]{3,2,1,0:T(8,128)(2,1)S(1)}, bf16[2,2,48,128]{3,2,1,0:T(8,128)(2,1)S(1)}, u32[]{:S(2)}, u32[]{:S(2)}) collective-permute-start(bf16[2,2,48,128]{3,2,1,0:T(8,128)(2,1)S(1)} %collective-permute-done.2), channel_id=1, source_target_pairs={{0,28},{4,0},{8,4},{12,8},{16,12},{20,16},{24,20},{28,24},{1,29},{... | collective-permute-start | bytes 147464 | tf_op jit(solution)/shard_map/ppermute | solution.py:18
  30.6 4.4 %collective-permute-start.1 = (bf16[2,2,48,128]{3,2,1,0:T(8,128)(2,1)S(1)}, bf16[2,2,48,128]{3,2,1,0:T(8,128)(2,1)S(1)}, u32[]{:S(2)}, u32[]{:S(2)}) collective-permute-start(bf16[2,2,48,128]{3,2,1,0:T(8,128)(2,1)S(1)} %collective-permute-done), channel_id=1, source_target_pairs={{0,4},{4,8},{8,12},{12,16},{16,20},{20,24},{24,28},{28,0},{1,5},{5... | collective-permute-start | bytes 147464 | tf_op jit(solution)/shard_map/ppermute | solution.py:18
  35.9 30.7 %copy-start.1 = (pred[6,2,5]{2,0,1:T(8,128)(4,1)S(1)}, pred[6,2,5]{2,0,1:T(8,128)(4,1)}, u32[]{:S(2)}) copy-start(pred[6,2,5]{2,0,1:T(8,128)(4,1)} %copy-done) | copy-start | bytes 184
where the time goes:
time: 166 us; the launch traced here: 165 us
  local copies, waits for them, and re-layouts  70 us (42%)
  blocking collectives  40.6 us (24%)
  matrix products  32.9 us (20%)
  starting transfers between devices  8.45 us (5%)
  other arithmetic  7.39 us (4%)
  waiting for transfers between devices  5.26 us (3%)
    all_gather x1, blocking collectives, per_device(): lax.all_gather(near_white, 'freq', axis=3, tiled=True)  27.1 us
    dynamic_update_slice x6, local copies, waits for them, and re-layouts, all_cross(): return lax.map(one_pair, (sources, receivers, source_masks, receiver_masks))  22.7 us
    broadcast_in_dim x6, local copies, waits for them, and re-layouts, all_cross(): return lax.map(one_pair, (sources, receivers, source_masks, receiver_masks))  22.4 us
    dot_general x6, matrix products, pair_cross(): jnp.einsum('ckfi,kfj->cfij', left_pair, right_part, preferred_element_typ...  15.8 us
    psum x1, blocking collectives, per_device(): energy = lax.psum(local_energy, 'freq') / total_bins  13.5 us
    dot_general x1, matrix products, per_device(): jnp.einsum('lk,pkn->pln', lag_cosines, flattened, preferred_element_type=...  13.1 us
    convert_element_type x1, local copies, waits for them, and re-layouts, per_device(): lagged.reshape(pairs_here, LAGS, row_count, block_width)  11 us
    ppermute x8, starting transfers between devices, from_behind(): return lax.ppermute(value, axis, pairs)  8.45 us
  transfers between devices with their start and end apart: 8, of which 4 were waited for; matrix products, arithmetic and copies ran while one was open for 3% of the time, Pallas kernels for 0%

commit v1 on v0

v1 whole, which is shorter than its diff:
```python
import functools
import math

import jax
import jax.numpy as jnp
import numpy as np
from jax import lax
from jax.experimental import pallas as pl
from jax.experimental.pallas import tpu as pltpu
from jax.sharding import PartitionSpec as P

REACH = 2
SPAN = 2 * REACH + 1
LAGS = 201
FINE = 8
COARSE = (LAGS + FINE - 1) // FINE
MESH = pl.DeviceIdType.MESH

epsilon = 1e-06


def gather_kernel(chan_count, freq_count, own_ref, mask_ref, near_ref, near_mask_ref,
                  local_sem, send_sem, recv_sem, mask_send_sem, mask_recv_sem):
    bins = own_ref.shape[2]
    me = lax.axis_index("chan")
    row = lax.axis_index("freq")
    sign = 1 - 2 * (me % 2)

    def chan_at(step):
        return (me + step + chan_count) % chan_count

    def freq_at(step):
        return (row + step) % freq_count

    def view(slot, shard):
        return near_ref.at[slot, :, :, pl.ds(pl.multiple_of(shard * bins, 16), bins), :]

    barrier = pltpu.get_barrier_semaphore()
    for step in (-2, -1, 1, 2):
        pl.semaphore_signal(barrier, inc=1, device_id=(chan_at(step), row), device_id_type=MESH)
    for step in range(1, freq_count):
        pl.semaphore_signal(barrier, inc=1, device_id=(me, freq_at(step)), device_id_type=MESH)
    local = pltpu.make_async_copy(own_ref, view(REACH, row), local_sem.at[0])
    local.start()
    local_mask = pltpu.make_async_copy(mask_ref, near_mask_ref.at[REACH], local_sem.at[1])
    local_mask.start()
    pl.semaphore_wait(barrier, 2 * REACH + freq_count - 1)

    sends = []

    def send(source, slot, shard, chan, freq):
        copy = pltpu.make_async_remote_copy(
            src_ref=source,
            dst_ref=view(slot, shard),
            send_sem=send_sem.at[len(sends)],
            recv_sem=recv_sem.at[slot, shard],
            device_id=(chan, freq),
            device_id_type=MESH,
        )
        copy.start()
        sends.append(copy)

    def await_shard(slot, shard):
        pltpu.make_async_remote_copy(
            src_ref=own_ref,
            dst_ref=view(slot, shard),
            send_sem=send_sem.at[0],
            recv_sem=recv_sem.at[slot, shard],
            device_id=(chan_at(1), row),
            device_id_type=MESH,
        ).wait_recv()

    def spread(source, shard):
        send(source, REACH - 2 * sign, shard, chan_at(2 * sign), row)
        send(source, REACH + sign, shard, chan_at(-sign), row)
        send(source, REACH - sign, shard, chan_at(sign), row)

    def relay(shard):
        await_shard(REACH - sign, shard)
        send(view(REACH - sign, shard), REACH - 2 * sign, shard, chan_at(sign), row)

    for step in range(1, freq_count):
        send(own_ref, REACH, row, me, freq_at(step))
    spread(own_ref, row)
    mask_copies = []
    for step in (-2, -1, 1, 2):
        copy = pltpu.make_async_remote_copy(
            src_ref=mask_ref,
            dst_ref=near_mask_ref.at[REACH - step],
            send_sem=mask_send_sem.at[REACH + step],
            recv_sem=mask_recv_sem.at[REACH - step],
            device_id=(chan_at(step), row),
            device_id_type=MESH,
        )
        copy.start()
        mask_copies.append(copy)
    for step in range(1, freq_count):
        shard = freq_at(step)
        await_shard(REACH, shard)
        spread(view(REACH, shard), shard)
        relay(freq_at(step - 1))
    relay(freq_at(freq_count - 1))
    for step in range(freq_count):
        shard = freq_at(step)
        await_shard(REACH + sign, shard)
        await_shard(REACH - 2 * sign, shard)
        await_shard(REACH + 2 * sign, shard)
    for copy in mask_copies:
        copy.wait_recv()
    for copy in mask_copies + sends:
        copy.wait_send()
    local.wait()
    local_mask.wait()


def gather_near(spectra, masks, chan_count, freq_count):
    parts, segments, bins, width = spectra.shape
    any_spec = pl.BlockSpec(memory_space=pl.ANY)
    return pl.pallas_call(
        functools.partial(gather_kernel, chan_count, freq_count),
        out_shape=(
            jax.ShapeDtypeStruct((SPAN, parts, segments, bins * freq_count, width), spectra.dtype),
            jax.ShapeDtypeStruct((SPAN,) + masks.shape, masks.dtype),
        ),
        in_specs=[any_spec, any_spec],
        out_specs=(any_spec, any_spec),
        scratch_shapes=[
            pltpu.SemaphoreType.DMA((2,)),
            pltpu.SemaphoreType.DMA((5 * freq_count - 1,)),
            pltpu.SemaphoreType.DMA((SPAN, freq_count)),
            pltpu.SemaphoreType.DMA((SPAN,)),
            pltpu.SemaphoreType.DMA((SPAN,)),
        ],
        compiler_params=pltpu.CompilerParams(collective_id=0, has_side_effects=True),
        name="gather_near",
    )(spectra, masks)


def correlate_kernel(chan_count, rows, pairs_ref, near_ref, mask_ref, coarse_ref, fine_ref,
                     out_ref, white, fine_wide, turned, count_rows, left, right):
    pair = pl.program_id(0)
    _, parts, segments, bins, width = near_ref.shape
    depth = parts * segments * bins
    half = depth // 2
    me = lax.axis_index("chan")
    row_first = pl.multiple_of(lax.axis_index("freq") * rows, 8)

    @pl.when(pair == 0)
    def _():
        @pl.loop(0, SPAN)
        def _(slot):
            for segment in range(segments):
                real = near_ref[slot, 0, segment].astype(jnp.float32)
                imag = near_ref[slot, 1, segment].astype(jnp.float32)
                energy = jnp.sum(real * real + imag * imag, axis=0, keepdims=True) / bins
                mask = mask_ref[slot, segment : segment + 1, :].astype(jnp.float32)
                weight = mask / jnp.sqrt(energy + epsilon)
                white[slot, 0, segment] = (real * weight).astype(jnp.bfloat16)
                white[slot, 1, segment] = (imag * weight).astype(jnp.bfloat16)

        for step in range(1, FINE):
            for part in range(2):
                column = part * FINE + step
                fine_wide[step, part] = jnp.broadcast_to(
                    fine_ref[:, column : column + 1], (bins, width)
                )

    def slot_of(side):
        return (pairs_ref[pair, side] - me + REACH + chan_count) % chan_count

    source_slot = slot_of(0)
    receiver_slot = slot_of(1)

    source = white[source_slot].reshape(depth, width).astype(jnp.float32)
    turned[...] = source.T
    straight = turned[pl.ds(row_first, rows), :]
    crossed = jnp.concatenate([-straight[:, half:], straight[:, :half]], axis=1)
    for step in range(COARSE):
        mixed = (
            straight * coarse_ref[0, step : step + 1, :]
            + crossed * coarse_ref[1, step : step + 1, :]
        )
        left[step] = mixed.astype(left.dtype)

    live = jnp.zeros((rows, width), jnp.float32)
    for segment in range(segments):
        source_mask = mask_ref[source_slot, segment : segment + 1, :].astype(jnp.float32)
        receiver_mask = mask_ref[receiver_slot, segment : segment + 1, :].astype(jnp.float32)
        count_rows[segment] = jnp.broadcast_to(source_mask, (width, width)).T
        live = live + count_rows[segment, pl.ds(row_first, rows), :] * receiver_mask
    scale = (1.0 / math.sqrt(bins)) / jnp.maximum(live, 1.0)

    for segment in range(segments):
        real = white[receiver_slot, 0, segment]
        imag = white[receiver_slot, 1, segment]
        first = segment * bins
        right[0, first : first + bins, :width] = real
        right[0, half + first : half + first + bins, :width] = imag
        real = real.astype(jnp.float32)
        imag = imag.astype(jnp.float32)
        for step in range(1, FINE):
            cosine = fine_wide[step, 0]
            sine = fine_wide[step, 1]
            lanes = slice((step % 2) * width, (step % 2 + 1) * width)
            right[step // 2, first : first + bins, lanes] = (
                cosine * real + sine * imag
            ).astype(jnp.bfloat16)
            right[step // 2, half + first : half + first + bins, lanes] = (
                cosine * imag - sine * real
            ).astype(jnp.bfloat16)

    @pl.loop(0, FINE // 2)
    def _(fine_pair):
        block = right[fine_pair]
        lhs = left[: COARSE - 1].reshape((COARSE - 1) * rows, depth).astype(jnp.bfloat16)
        product = jnp.dot(lhs, block, preferred_element_type=jnp.float32)
        for step in range(COARSE - 1):
            for side in range(2):
                part = product[step * rows : (step + 1) * rows, side * width : (side + 1) * width]
                out_ref[0, step * FINE + 2 * fine_pair + side] = (part * scale).astype(out_ref.dtype)

    last = jnp.dot(
        left[COARSE - 1].astype(jnp.bfloat16), right[0, :, :width],
        preferred_element_type=jnp.float32,
    )
    out_ref[0, LAGS - 1] = (last * scale).astype(out_ref.dtype)


def angle_tables(bins, repeats):
    ids = np.arange(bins)
    coarse = (np.arange(COARSE)[:, None] * FINE - LAGS // 2) * ids[None, :] % (2 * bins)
    coarse = np.tile(coarse * (math.pi / bins), (1, repeats))
    fine = (np.arange(FINE)[None, :] * ids[:, None]) % (2 * bins) * (math.pi / bins)
    return (
        np.stack([np.cos(coarse), np.sin(coarse)]).astype(np.float32),
        np.concatenate([np.cos(fine), np.sin(fine)], axis=1).astype(np.float32),
    )


def correlate(pair_blocks, near, near_masks, chan_count, rows):
    _, parts, segments, bins, width = near.shape
    depth = parts * segments * bins
    pairs = pair_blocks.shape[0]
    coarse, fine = angle_tables(bins, parts * segments)
    left_type = jnp.bfloat16 if rows % 16 == 0 else jnp.float32
    return pl.pallas_call(
        functools.partial(correlate_kernel, chan_count, rows),
        out_shape=jax.ShapeDtypeStruct((pairs, LAGS, rows, width), jnp.bfloat16),
        grid=(pairs,),
        in_specs=[
            pl.BlockSpec(memory_space=pltpu.SMEM),
            pl.BlockSpec(near.shape, lambda p: (0,) * 5),
            pl.BlockSpec(near_masks.shape, lambda p: (0,) * 3),
            pl.BlockSpec(coarse.shape, lambda p: (0,) * 3),
            pl.BlockSpec(fine.shape, lambda p: (0,) * 2),
        ],
        out_specs=pl.BlockSpec((1, LAGS, rows, width), lambda p: (p, 0, 0, 0)),
        scratch_shapes=[
            pltpu.VMEM(near.shape, jnp.bfloat16),
            pltpu.VMEM((FINE, 2, bins, width), jnp.float32),
            pltpu.VMEM((width, depth), jnp.float32),
            pltpu.VMEM((segments, width, width), jnp.float32),
            pltpu.VMEM((COARSE, rows, depth), left_type),
            pltpu.VMEM((FINE // 2, depth, 2 * width), jnp.bfloat16),
        ],
        compiler_params=pltpu.CompilerParams(
            dimension_semantics=("arbitrary",), vmem_limit_bytes=56 * 1024 * 1024
        ),
        name="correlate",
    )(pair_blocks, near, near_masks, jnp.asarray(coarse), jnp.asarray(fine))


def per_device(chan_count, freq_count, spectra, masks, pair_blocks):
    near, near_masks = gather_near(spectra, masks, chan_count, freq_count)
    rows = spectra.shape[3] // freq_count
    return correlate(pair_blocks, near, near_masks, chan_count, rows)


def solution(mesh):
    return jax.shard_map(
        functools.partial(per_device, mesh.shape["chan"], mesh.shape["freq"]),
        mesh=mesh,
        in_specs=(P(None, None, "freq", "chan"), P(None, "chan"), P("chan", None)),
        out_specs=P("chan", None, "freq", None),
        check_vma=False,
    )
```

time: 166 us -> 44.6 us (0.27)
  local copies, waits for them, and re-layouts: 70 us -> 1.35 us
  Pallas kernels: 0 us -> 43 us
  blocking collectives: 40.6 us -> 0 us
  matrix products: 32.9 us -> 0 us
  starting transfers between devices: 8.45 us -> 0 us
  other arithmetic: 7.39 us -> 0 us
  waiting for transfers between devices: 5.26 us -> 0 us
    pallas_call x0 -> x2, Pallas kernels: none -> 43 us  [the longest x1 23 us: correlate(): pl.pallas_call(functools.partial(correlate_kernel, chan_count, rows), out...]
    dot_general x17 -> x0, matrix products: 32.9 us -> none  [the longest x6 15.8 us: pair_cross(): jnp.einsum('ckfi,kfj->cfij', left_pair, right_part, preferred_element_typ...]
    all_gather x1 -> x0, blocking collectives: 27.1 us -> none  [per_device(): lax.all_gather(near_white, 'freq', axis=3, tiled=True)]
    dynamic_update_slice x6 -> x0, local copies, waits for them, and re-layouts: 22.7 us -> none  [all_cross(): return lax.map(one_pair, (sources, receivers, source_masks, receiver_masks))]
    broadcast_in_dim x6 -> x0, local copies, waits for them, and re-layouts: 22.4 us -> none  [all_cross(): return lax.map(one_pair, (sources, receivers, source_masks, receiver_masks))]
    psum x1 -> x0, blocking collectives: 13.5 us -> none  [per_device(): energy = lax.psum(local_energy, 'freq') / total_bins]
    convert_element_type x1 -> x0, local copies, waits for them, and re-layouts: 11 us -> none  [per_device(): lagged.reshape(pairs_here, LAGS, row_count, block_width)]
    ppermute x8 -> x0, starting transfers between devices: 8.45 us -> none  [from_behind(): return lax.ppermute(value, axis, pairs)]
  transfers between devices with their start and end apart: 8 -> 0, of which waited for: 4 -> 0; matrix products, arithmetic and copies ran while one was open for 3% -> 0% of each run, Pallas kernels for 0% -> 0%
where the time goes in v1:
time: 44.6 us; the launch traced here: 44.4 us
  Pallas kernels  43 us (96%)
  local copies, waits for them, and re-layouts  1.35 us (3%)
    pallas_call x1, Pallas kernels, correlate(): pl.pallas_call(functools.partial(correlate_kernel, chan_count, rows), out...  23 us
    pallas_call x1, Pallas kernels, gather_near(): pl.pallas_call(functools.partial(gather_kernel, chan_count, freq_count),...  20 us
    unnamed x1, local copies, waits for them, and re-layouts  1.35 us

profile of v1, /device:TPU:0, one launch (start us, length us, event | category | flops | bytes accessed | tf_op | source)
XLA Modules:
  0.0 44.4 jit_solution(13474698267155338775)
XLA Ops:
  0.0 1.4 %copy.6.pairs_ref = s32[6,2]{1,0:T(8,128)} copy(s32[6,2]{0,1:T(2,128)} %param.7) | data formatting | bytes 96 | tf_op args[2]
  1.4 20.0 %gather_near.1 = (bf16[5,2,2,192,128]{4,3,2,1,0:T(8,128)(2,1)}, s32[5,2,128]{2,1,0:T(2,128)}) custom-call(bf16[2,2,48,128]{3,2,1,0:T(8,128)(2,1)} %own_ref.1, s32[2,128]{1,0:T(2,128)} %mask_ref.1), custom_call_target="tpu_custom_call" | custom-call | tf_op jit(solution)/shard_map/gather_near/pallas_call | solution.py:119
  21.4 23.0 %correlate.1 = bf16[6,201,32,128]{3,2,1,0:T(8,128)(2,1)} custom-call(s32[6,2]{1,0:T(8,128)} %copy.6.pairs_ref, bf16[5,2,2,192,128]{4,3,2,1,0:T(8,128)(2,1)} %get-tuple-element.7.near_ref, s32[5,2,128]{2,1,0:T(2,128)} %get-tuple-element.8.mask_ref, f32[2,26,768]{2,1,0:T(8,128)} %constant.4.clone.coarse_ref, f32[192,16]{1,0:T(8,128)} %constant.5.clone.fine_ref), custom_call_target="tpu_custom_call" | custom-call | tf_op jit(solution)/shard_map/correlate/pallas_call | solution.py:246

commit v2 on v1

--- a/solution.py
+++ b/solution.py
@@ -13,7 +13,10 @@
 SPAN = 2 * REACH + 1
 LAGS = 201
 FINE = 8
-COARSE = (LAGS + FINE - 1) // FINE
+FINE_SIDE = FINE // 2
+COARSE_SIDE = LAGS // 2 // FINE
+COARSE = 2 * COARSE_SIDE + 1
+DIRECT = (0, 1)
 MESH = pl.DeviceIdType.MESH
 
 epsilon = 1e-06
@@ -35,16 +38,24 @@
     def view(slot, shard):
         return near_ref.at[slot, :, :, pl.ds(pl.multiple_of(shard * bins, 16), bins), :]
 
+    direct = [step for step in DIRECT if step < freq_count]
+    direct += [freq_count - step for step in direct if step not in (0, freq_count - step)]
     barrier = pltpu.get_barrier_semaphore()
     for step in (-2, -1, 1, 2):
         pl.semaphore_signal(barrier, inc=1, device_id=(chan_at(step), row), device_id_type=MESH)
     for step in range(1, freq_count):
         pl.semaphore_signal(barrier, inc=1, device_id=(me, freq_at(step)), device_id_type=MESH)
+    for step in direct[1:]:
+        for back in (-2 * sign, -sign):
+            pl.semaphore_signal(
+                barrier, inc=1, device_id=(chan_at(back), freq_at(freq_count - step)),
+                device_id_type=MESH,
+            )
     local = pltpu.make_async_copy(own_ref, view(REACH, row), local_sem.at[0])
     local.start()
     local_mask = pltpu.make_async_copy(mask_ref, near_mask_ref.at[REACH], local_sem.at[1])
     local_mask.start()
-    pl.semaphore_wait(barrier, 2 * REACH + freq_count - 1)
+    pl.semaphore_wait(barrier, 2 * REACH + freq_count - 1 + 2 * len(direct[1:]))
 
     sends = []
 
@@ -70,18 +81,24 @@
             device_id_type=MESH,
         ).wait_recv()
 
-    def spread(source, shard):
-        send(source, REACH - 2 * sign, shard, chan_at(2 * sign), row)
-        send(source, REACH + sign, shard, chan_at(-sign), row)
+    def spread(source, shard, freq):
+        send(source, REACH - 2 * sign, shard, chan_at(2 * sign), freq)
+        send(source, REACH + sign, shard, chan_at(-sign), freq)
+
+    def to_partner(source, shard):
         send(source, REACH - sign, shard, chan_at(sign), row)
 
     def relay(shard):
         await_shard(REACH - sign, shard)
         send(view(REACH - sign, shard), REACH - 2 * sign, shard, chan_at(sign), row)
 
-    for step in range(1, freq_count):
+    chained = [step for step in range(1, freq_count) if step not in direct]
+    steps = direct[1:] + chained
+    for step in chained + direct[1:]:
         send(own_ref, REACH, row, me, freq_at(step))
-    spread(own_ref, row)
+    for step in direct:
+        spread(own_ref, row, freq_at(step))
+    to_partner(own_ref, row)
     mask_copies = []
     for step in (-2, -1, 1, 2):
         copy = pltpu.make_async_remote_copy(
@@ -94,12 +111,18 @@
         )
         copy.start()
         mask_copies.append(copy)
-    for step in range(1, freq_count):
+    for step in chained:
         shard = freq_at(step)
         await_shard(REACH, shard)
-        spread(view(REACH, shard), shard)
-        relay(freq_at(step - 1))
-    relay(freq_at(freq_count - 1))
+        spread(view(REACH, shard), shard, row)
+        to_partner(view(REACH, shard), shard)
+    relay(row)
+    for step in direct[1:]:
+        shard = freq_at(step)
+        await_shard(REACH, shard)
+        to_partner(view(REACH, shard), shard)
+    for step in steps:
+        relay(freq_at(step))
     for step in range(freq_count):
         shard = freq_at(step)
         await_shard(REACH + sign, shard)
@@ -137,13 +160,80 @@
 
 
 def correlate_kernel(chan_count, rows, pairs_ref, near_ref, mask_ref, coarse_ref, fine_ref,
-                     out_ref, white, fine_wide, turned, count_rows, left, right):
+                     out_ref, white, fine_wide, turned, count_rows, near_scale,
+                     left_even, left_odd, right_even, right_odd, beyond_even, beyond_odd):
     pair = pl.program_id(0)
+    pairs = pl.num_programs(0)
     _, parts, segments, bins, width = near_ref.shape
     depth = parts * segments * bins
     half = depth // 2
     me = lax.axis_index("chan")
     row_first = pl.multiple_of(lax.axis_index("freq") * rows, 8)
+
+    def slot_of(side, which):
+        return (pairs_ref[side, which] - me + REACH + chan_count) % chan_count
+
+    def begin(which, parity):
+        source_slot = slot_of(0, which)
+        receiver_slot = slot_of(1, which)
+        source = white[source_slot].reshape(depth, width).astype(jnp.float32)
+        turned[...] = source.T
+        live = jnp.zeros((rows, width), jnp.float32)
+        for segment in range(segments):
+            source_mask = mask_ref[source_slot, segment : segment + 1, :].astype(jnp.float32)
+            receiver_mask = mask_ref[receiver_slot, segment : segment + 1, :].astype(jnp.float32)
+            count_rows[segment] = jnp.broadcast_to(source_mask, (width, width)).T
+            live = live + count_rows[segment, pl.ds(row_first, rows), :] * receiver_mask
+        near_scale[parity] = (1.0 / math.sqrt(bins)) / jnp.maximum(live, 1.0)
+        return receiver_slot
+
+    def modulate(receiver_slot, left, right, beyond):
+        straight = turned[pl.ds(row_first, rows), :]
+        crossed = jnp.concatenate([-straight[:, half:], straight[:, :half]], axis=1)
+        left[COARSE_SIDE] = straight.astype(left.dtype)
+        for step in range(1, COARSE_SIDE + 1):
+            cosine = straight * coarse_ref[0, step : step + 1, :]
+            sine = crossed * coarse_ref[1, step : step + 1, :]
+            left[COARSE_SIDE + step] = (cosine + sine).astype(left.dtype)
+            left[COARSE_SIDE - step] = (cosine - sine).astype(left.dtype)
+        for segment in range(segments):
+            real = white[receiver_slot, 0, segment]
+            imag = white[receiver_slot, 1, segment]
+            real_rows = slice(segment * bins, (segment + 1) * bins)
+            imag_rows = slice(half + segment * bins, half + (segment + 1) * bins)
+
+            def put(fine, new_real, new_imag):
+                if fine == FINE_SIDE:
+                    beyond[real_rows, :] = new_real.astype(jnp.bfloat16)
+                    beyond[imag_rows, :] = new_imag.astype(jnp.bfloat16)
+                else:
+                    first = (fine + FINE_SIDE) * width
+                    right[real_rows, first : first + width] = new_real.astype(jnp.bfloat16)
+                    right[imag_rows, first : first + width] = new_imag.astype(jnp.bfloat16)
+
+            put(0, real, imag)
+            real = real.astype(jnp.float32)
+            imag = imag.astype(jnp.float32)
+            for step in range(1, FINE_SIDE + 1):
+                cosine = fine_wide[step, 0]
+                sine = fine_wide[step, 1]
+                real_cosine, real_sine = cosine * real, sine * real
+                imag_cosine, imag_sine = cosine * imag, sine * imag
+                put(step, real_cosine + imag_sine, imag_cosine - real_sine)
+                put(-step, real_cosine - imag_sine, imag_cosine + real_sine)
+
+    def multiply(left, right, beyond, scale):
+        lhs = left[...].reshape(COARSE * rows, depth).astype(jnp.bfloat16)
+        product = jnp.dot(lhs, right[...], preferred_element_type=jnp.float32)
+        for step in range(COARSE):
+            for side in range(FINE):
+                part = product[step * rows : (step + 1) * rows, side * width : (side + 1) * width]
+                out_ref[0, step * FINE + side] = (part * scale).astype(out_ref.dtype)
+        last = jnp.dot(
+            left[COARSE - 1].astype(jnp.bfloat16), beyond[...],
+            preferred_element_type=jnp.float32,
+        )
+        out_ref[0, LAGS - 1] = (last * scale).astype(out_ref.dtype)
 
     @pl.when(pair == 0)
     def _():
@@ -158,79 +248,37 @@
                 white[slot, 0, segment] = (real * weight).astype(jnp.bfloat16)
                 white[slot, 1, segment] = (imag * weight).astype(jnp.bfloat16)
 
-        for step in range(1, FINE):
+        for step in range(1, FINE_SIDE + 1):
             for part in range(2):
-                column = part * FINE + step
+                column = part * (FINE_SIDE + 1) + step
                 fine_wide[step, part] = jnp.broadcast_to(
                     fine_ref[:, column : column + 1], (bins, width)
                 )
 
-    def slot_of(side):
-        return (pairs_ref[pair, side] - me + REACH + chan_count) % chan_count
-
-    source_slot = slot_of(0)
-    receiver_slot = slot_of(1)
-
-    source = white[source_slot].reshape(depth, width).astype(jnp.float32)
-    turned[...] = source.T
-    straight = turned[pl.ds(row_first, rows), :]
-    crossed = jnp.concatenate([-straight[:, half:], straight[:, :half]], axis=1)
-    for step in range(COARSE):
-        mixed = (
-            straight * coarse_ref[0, step : step + 1, :]
-            + crossed * coarse_ref[1, step : step + 1, :]
-        )
-        left[step] = mixed.astype(left.dtype)
-
-    live = jnp.zeros((rows, width), jnp.float32)
-    for segment in range(segments):
-        source_mask = mask_ref[source_slot, segment : segment + 1, :].astype(jnp.float32)
-        receiver_mask = mask_ref[receiver_slot, segment : segment + 1, :].astype(jnp.float32)
-        count_rows[segment] = jnp.broadcast_to(source_mask, (width, width)).T
-        live = live + count_rows[segment, pl.ds(row_first, rows), :] * receiver_mask
-    scale = (1.0 / math.sqrt(bins)) / jnp.maximum(live, 1.0)
-
-    for segment in range(segments):
-        real = white[receiver_slot, 0, segment]
-        imag = white[receiver_slot, 1, segment]
-        first = segment * bins
-        right[0, first : first + bins, :width] = real
-        right[0, half + first : half + first + bins, :width] = imag
-        real = real.astype(jnp.float32)
-        imag = imag.astype(jnp.float32)
-        for step in range(1, FINE):
-            cosine = fine_wide[step, 0]
-            sine = fine_wide[step, 1]
-            lanes = slice((step % 2) * width, (step % 2 + 1) * width)
-            right[step // 2, first : first + bins, lanes] = (
-                cosine * real + sine * imag
-            ).astype(jnp.bfloat16)
-            right[step // 2, half + first : half + first + bins, lanes] = (
-                cosine * imag - sine * real
-            ).astype(jnp.bfloat16)
-
-    @pl.loop(0, FINE // 2)
-    def _(fine_pair):
-        block = right[fine_pair]
-        lhs = left[: COARSE - 1].reshape((COARSE - 1) * rows, depth).astype(jnp.bfloat16)
-        product = jnp.dot(lhs, block, preferred_element_type=jnp.float32)
-        for step in range(COARSE - 1):
-            for side in range(2):
-                part = product[step * rows : (step + 1) * rows, side * width : (side + 1) * width]
-                out_ref[0, step * FINE + 2 * fine_pair + side] = (part * scale).astype(out_ref.dtype)
-
-    last = jnp.dot(
-        left[COARSE - 1].astype(jnp.bfloat16), right[0, :, :width],
-        preferred_element_type=jnp.float32,
-    )
-    out_ref[0, LAGS - 1] = (last * scale).astype(out_ref.dtype)
+        modulate(begin(0, 0), left_even, right_even, beyond_even)
+
+    def one_pair(parity, ours, others):
+        receiver_slot = begin(jnp.minimum(pair + 1, pairs - 1), 1 - parity)
+        modulate(receiver_slot, *others)
+        multiply(*ours, near_scale[parity])
+
+    even = (left_even, right_even, beyond_even)
+    odd = (left_odd, right_odd, beyond_odd)
+
+    @pl.when(pair % 2 == 0)
+    def _():
+        one_pair(0, even, odd)
+
+    @pl.when(pair % 2 == 1)
+    def _():
+        one_pair(1, odd, even)
 
 
 def angle_tables(bins, repeats):
     ids = np.arange(bins)
-    coarse = (np.arange(COARSE)[:, None] * FINE - LAGS // 2) * ids[None, :] % (2 * bins)
+    coarse = np.arange(COARSE_SIDE + 1)[:, None] * FINE * ids[None, :] % (2 * bins)
     coarse = np.tile(coarse * (math.pi / bins), (1, repeats))
-    fine = (np.arange(FINE)[None, :] * ids[:, None]) % (2 * bins) * (math.pi / bins)
+    fine = np.arange(FINE_SIDE + 1)[None, :] * ids[:, None] % (2 * bins) * (math.pi / bins)
     return (
         np.stack([np.cos(coarse), np.sin(coarse)]).astype(np.float32),
         np.concatenate([np.cos(fine), np.sin(fine)], axis=1).astype(np.float32),
@@ -257,17 +305,22 @@
         out_specs=pl.BlockSpec((1, LAGS, rows, width), lambda p: (p, 0, 0, 0)),
         scratch_shapes=[
             pltpu.VMEM(near.shape, jnp.bfloat16),
-            pltpu.VMEM((FINE, 2, bins, width), jnp.float32),
+            pltpu.VMEM((FINE_SIDE + 1, 2, bins, width), jnp.float32),
             pltpu.VMEM((width, depth), jnp.float32),
             pltpu.VMEM((segments, width, width), jnp.float32),
+            pltpu.VMEM((2, rows, width), jnp.float32),
             pltpu.VMEM((COARSE, rows, depth), left_type),
-            pltpu.VMEM((FINE // 2, depth, 2 * width), jnp.bfloat16),
+            pltpu.VMEM((COARSE, rows, depth), left_type),
+            pltpu.VMEM((depth, FINE * width), jnp.bfloat16),
+            pltpu.VMEM((depth, FINE * width), jnp.bfloat16),
+            pltpu.VMEM((depth, width), jnp.bfloat16),
+            pltpu.VMEM((depth, width), jnp.bfloat16),
         ],
         compiler_params=pltpu.CompilerParams(
             dimension_semantics=("arbitrary",), vmem_limit_bytes=56 * 1024 * 1024
         ),
         name="correlate",
-    )(pair_blocks, near, near_masks, jnp.asarray(coarse), jnp.asarray(fine))
+    )(pair_blocks.T, near, near_masks, jnp.asarray(coarse), jnp.asarray(fine))
 
 
 def per_device(chan_count, freq_count, spectra, masks, pair_blocks):

time: 44.6 us -> 37.8 us (0.85)
  Pallas kernels: 43 us -> 37.7 us
  local copies, waits for them, and re-layouts: 1.35 us -> 0 us
    pallas_call x1, Pallas kernels: 23 us -> 18.9 us  [correlate(): pl.pallas_call(functools.partial(correlate_kernel, chan_count, rows), out...]
    unnamed x1 -> x0, local copies, waits for them, and re-layouts: 1.35 us -> none
    pallas_call x1, Pallas kernels: 20 us -> 18.8 us  [gather_near(): pl.pallas_call(functools.partial(gather_kernel, chan_count, freq_count),...]
where the time goes in v2:
time: 37.8 us; the launch traced here: 37.7 us
  Pallas kernels  37.7 us (100%)
    pallas_call x1, Pallas kernels, correlate(): pl.pallas_call(functools.partial(correlate_kernel, chan_count, rows), out...  18.9 us
    pallas_call x1, Pallas kernels, gather_near(): pl.pallas_call(functools.partial(gather_kernel, chan_count, freq_count),...  18.8 us

profile of v2, /device:TPU:0, one launch (start us, length us, event | category | flops | bytes accessed | tf_op | source)
XLA Modules:
  0.0 37.7 jit_solution(7422321820738393109)
XLA Ops:
  0.0 18.8 %gather_near.1 = (bf16[5,2,2,192,128]{4,3,2,1,0:T(8,128)(2,1)}, s32[5,2,128]{2,1,0:T(2,128)}) custom-call(bf16[2,2,48,128]{3,2,1,0:T(8,128)(2,1)} %own_ref.1, s32[2,128]{1,0:T(2,128)} %mask_ref.1), custom_call_target="tpu_custom_call" | custom-call | tf_op jit(solution)/shard_map/gather_near/pallas_call | solution.py:142
  18.8 18.9 %correlate.1 = bf16[6,201,32,128]{3,2,1,0:T(8,128)(2,1)} custom-call(s32[2,6]{1,0:T(2,128)} %bitcast.1, bf16[5,2,2,192,128]{4,3,2,1,0:T(8,128)(2,1)} %get-tuple-element.7.near_ref, s32[5,2,128]{2,1,0:T(2,128)} %get-tuple-element.8.mask_ref, f32[2,13,768]{2,1,0:T(8,128)} %constant.4.clone.coarse_ref, f32[192,10]{1,0:T(8,128)} %constant.5.clone.fine_ref), custom_call_target="tpu_custom_call" | custom-call | tf_op jit(solution)/shard_map/correlate/pallas_call | solution.py:294

commit v3 on v2

--- a/solution.py
+++ b/solution.py
@@ -258,8 +258,10 @@
         modulate(begin(0, 0), left_even, right_even, beyond_even)
 
     def one_pair(parity, ours, others):
-        receiver_slot = begin(jnp.minimum(pair + 1, pairs - 1), 1 - parity)
-        modulate(receiver_slot, *others)
+        @pl.when(pair + 1 < pairs)
+        def _():
+            modulate(begin(pair + 1, 1 - parity), *others)
+
         multiply(*ours, near_scale[parity])
 
     even = (left_even, right_even, beyond_even)

time: 37.8 us -> 37.5 us (level)
  Pallas kernels: 37.7 us -> 37.3 us
where the time goes in v3:
time: 37.5 us; the launch traced here: 37.3 us
  Pallas kernels  37.3 us (99%)
    pallas_call x1, Pallas kernels, gather_near(): pl.pallas_call(functools.partial(gather_kernel, chan_count, freq_count),...  18.8 us
    pallas_call x1, Pallas kernels, correlate(): pl.pallas_call(functools.partial(correlate_kernel, chan_count, rows), out...  18.5 us

profile of v3, /device:TPU:0, one launch (start us, length us, event | category | flops | bytes accessed | tf_op | source)
XLA Modules:
  0.0 37.3 jit_solution(14321299634593099741)
XLA Ops:
  0.0 18.8 %gather_near.1 = (bf16[5,2,2,192,128]{4,3,2,1,0:T(8,128)(2,1)}, s32[5,2,128]{2,1,0:T(2,128)}) custom-call(bf16[2,2,48,128]{3,2,1,0:T(8,128)(2,1)} %own_ref.1, s32[2,128]{1,0:T(2,128)} %mask_ref.1), custom_call_target="tpu_custom_call" | custom-call | tf_op jit(solution)/shard_map/gather_near/pallas_call | solution.py:142
  18.8 18.5 %correlate.1 = bf16[6,201,32,128]{3,2,1,0:T(8,128)(2,1)} custom-call(s32[2,6]{1,0:T(2,128)} %bitcast.1, bf16[5,2,2,192,128]{4,3,2,1,0:T(8,128)(2,1)} %get-tuple-element.7.near_ref, s32[5,2,128]{2,1,0:T(2,128)} %get-tuple-element.8.mask_ref, f32[2,13,768]{2,1,0:T(8,128)} %constant.4.clone.coarse_ref, f32[192,10]{1,0:T(8,128)} %constant.5.clone.fine_ref), custom_call_target="tpu_custom_call" | custom-call | tf_op jit(solution)/shard_map/correlate/pallas_call | solution.py:296
